TPU v7x, 256 devices: a whole 4x4x8 slice. The times are simulated.
256 devices in a mesh: ctx: 16 (over x, y_hi, core), head: 16 (over z, y_lo).
Axes of the slice: x: 4, y: 4 (y_hi: 2, y_lo: 2; y = y_hi * 2 + y_lo), z: 8, core: 2. Of those that a mesh axis runs over, the one named last changes fastest.
Arguments:
- queries: bfloat16 [2048, 128, 128], P('ctx', 'head'), may hold values from -6 to 6
- query_rope: bfloat16 [2048, 128, 64], P('ctx', 'head'), may hold values from -100 to 100
- latent_cache: bfloat16 [2048, 576], P('ctx'), may hold values from -8 to 8
- key_up: bfloat16 [512, 16384], P(None, 'head'), may hold values from -0.25 to 0.25
- value_up: bfloat16 [512, 16384], P(None, 'head'), may hold values from -0.25 to 0.25
- out_proj: bfloat16 [16384, 7168], P('head', 'ctx'), may hold values from -0.75 to 0.75
Outputs:
- mixed_out: bfloat16 [2048, 7168], P(('ctx', 'head'))
All inputs are finite; a program needn't handle non-finite values.
Results may differ from a plain program's by a relative error of at most 0.024.
Values may be sent and summed in bfloat16 or wider, within the bound.
A program may use at most 64 MiB of HBM per device.

v0:
```python
import jax
import jax.numpy as jnp
from jax import lax
from jax.sharding import PartitionSpec as P

LAT = 512
ROPE = 64
NOPE = 128
VD = 128


MASKED = -1e30


def shifted(shard, axis, by):
    count = lax.axis_size(axis)
    pairs = [(i, i + by) for i in range(count) if 0 <= i + by < count]
    return lax.ppermute(shard, axis, pairs)


def attend(state, cache_block, offset, first_query, queries, query_rope, key_up, value_up):
    running_max, weight_sum, weighted = state
    row_total = cache_block.shape[0]
    query_total = queries.shape[0]
    head_count = queries.shape[1]
    latent = cache_block[:, :LAT]
    rope_keys = cache_block[:, LAT:]
    key_rows = (
        jnp.dot(latent, key_up, preferred_element_type=jnp.float32)
        .astype(jnp.bfloat16)
        .reshape(row_total, head_count, NOPE)
    )
    value_rows = (
        jnp.dot(latent, value_up, preferred_element_type=jnp.float32)
        .astype(jnp.bfloat16)
        .reshape(row_total, head_count, VD)
    )
    scores = jnp.einsum("qhd,khd->qhk", queries, key_rows, preferred_element_type=jnp.float32)
    scores = (
        scores
        + jnp.einsum("qhr,kr->qhk", query_rope, rope_keys, preferred_element_type=jnp.float32)
    ) * (NOPE + ROPE) ** (-0.5)
    query_pos = first_query + lax.broadcasted_iota(jnp.int32, (query_total, 1, row_total), 0)
    key_pos = offset + lax.broadcasted_iota(jnp.int32, (query_total, 1, row_total), 2)
    scores = jnp.where(key_pos <= query_pos, scores, MASKED)
    new_max = jnp.maximum(running_max, jnp.max(scores, axis=2))
    exps = jnp.exp(scores - new_max[:, :, None])
    rescale = jnp.exp(running_max - new_max)
    weight_sum = weight_sum * rescale + jnp.sum(exps, axis=2)
    weighted = weighted * rescale[:, :, None] + jnp.einsum(
        "qhk,khv->qhv", exps.astype(jnp.bfloat16), value_rows, preferred_element_type=jnp.float32
    )
    return (new_max, weight_sum, weighted)


def local(queries, query_rope, latent_cache, key_up, value_up, out_proj):
    row_count = queries.shape[0]
    head_count = queries.shape[1]
    ctx_count = lax.axis_size("ctx")
    own_index = lax.axis_index("ctx")
    first_query = own_index * row_count
    start_state = (
        jnp.full((row_count, head_count), MASKED, jnp.float32),
        jnp.zeros((row_count, head_count), jnp.float32),
        jnp.zeros((row_count, head_count, VD), jnp.float32),
    )

    def visit(state, cache_block, offset):
        return lax.cond(
            offset <= first_query,
            lambda kept_state: attend(
                kept_state, cache_block, offset, first_query, queries, query_rope, key_up, value_up
            ),
            lambda kept_state: kept_state,
            state,
        )

    def cycle_turn(turn_index, carry):
        state, cache_block = carry
        source = (own_index - turn_index) % ctx_count
        state = visit(state, cache_block, source * row_count)
        cache_block = shifted(cache_block, "ctx", 1)
        return (state, cache_block)

    state, cache_block = lax.fori_loop(0, ctx_count - 1, cycle_turn, (start_state, latent_cache))
    state = visit(state, cache_block, (own_index + 1) % ctx_count * row_count)
    attention = (
        (state[2] / state[1][:, :, None]).astype(jnp.bfloat16).reshape(row_count, head_count * VD)
    )
    partial_sum = jnp.dot(
        attention,
        lax.all_gather(out_proj, "ctx", axis=1, tiled=True),
        preferred_element_type=jnp.float32,
    )
    mixed_out = lax.psum_scatter(
        partial_sum.astype(jnp.bfloat16), "head", scatter_dimension=0, tiled=True
    )
    return mixed_out


def solution(mesh):
    placed = (
        P("ctx", "head", None),
        P("ctx", "head", None),
        P("ctx", None),
        P(None, "head"),
        P(None, "head"),
        P("head", "ctx"),
    )
    return jax.shard_map(
        local, mesh=mesh, in_specs=placed, out_specs=P(("ctx", "head"), None), check_vma=False
    )
```

profile of v0, /device:TPU:2, one launch (start us, length us, event | category | flops | bytes accessed | tf_op | source)
XLA Modules:
  0.0 262.6 jit_solution(1126919409990677418)
XLA Ops:
  6.5 0.9 copy.57
  7.5 1.0 copy.13
  8.6 155.7 %while.21 = (s32[]{:T(128)}, f32[128,8]{0,1:T(8,128)S(1)}, f32[128,8]{0,1:T(8,128)S(1)}, f32[128,8,128]{0,2,1:T(8,128)S(1)}, bf16[128,576]{0,1:T(8,128)(2,1)S(1)...) while((s32[]{:T(128)}, f32[128,8]{0,1:T(8,128)S(1)}, ...), condition=%wide.region_5.6_spmd, body=%wide.region_0.5_spmd.sunk | while | flops 353913088 | bytes 8997344 | solution.py:85
  8.6 0.7 copy.46
  9.3 1.9 collective-permute-start
  11.2 5.6 %conditional.4 = ((f32[128,8]{0,1:T(8,128)S(1)}, f32[128,8]{0,1:T(8,128)S(1)}, f32[128,8,128]{0,2,1:T(8,128)S(1)})) conditional(s32[]{:T(128)} %convert_element_type.55, (f32[128,8]{0,1:T(8,128)S(1)}, f32[128,8]{0,1:T(8,128)S(1)}, f32[128,8,128]{0,2,1:T(8,128)S(1)}) %tuple.62, (s32[]{:T(128)}, s32[]{:T(128)}, bf16[128,576]{0,1:T(8,128)(2,1)}, ...), branch_computations={%region_1.1_spmd, %region_2.4_spmd} | conditional | flops 353913088 | bytes 8112168 | solution.py:69
  11.3 1.6 fusion.3
  13.3 1.2 fusion.29
  14.6 1.6 convolution_convert_fusion
  16.8 1.5 collective-permute-done
  18.4 0.7 copy.46
  19.0 3.7 %collective-permute-start = (bf16[128,576]{0,1:T(8,128)(2,1)}, bf16[128,576]{0,1:T(8,128)(2,1)S(1)}, u32[]{:S(2)}, u32[]{:S(2)}) collective-permute-start(bf16[128,576]{0,1:T(8,128)(2,1)} %copy.46), channel_id=1, source_target_pairs={{0,16},{16,32},{32,48},{48,64},{64,80},{80,96},{96,112},{112,128},... | collective-permute-start | bytes 442376 | tf_op jit(solution)/shard_map/while/body/eval_jaxpr/ppermute | solution.py:18
  22.7 5.7 %conditional.4 = ((f32[128,8]{0,1:T(8,128)S(1)}, f32[128,8]{0,1:T(8,128)S(1)}, f32[128,8,128]{0,2,1:T(8,128)S(1)})) conditional(s32[]{:T(128)} %convert_element_type.55, (f32[128,8]{0,1:T(8,128)S(1)}, f32[128,8]{0,1:T(8,128)S(1)}, f32[128,8,128]{0,2,1:T(8,128)S(1)}) %tuple.62, (s32[]{:T(128)}, s32[]{:T(128)}, bf16[128,576]{0,1:T(8,128)(2,1)}, ...), branch_computations={%region_1.1_spmd, %region_2.4_spmd} | conditional | flops 353913088 | bytes 8112168 | solution.py:69
  22.8 1.6 fusion.3
  24.8 1.2 fusion.29
  26.1 1.7 convolution_convert_fusion
  28.4 0.7 copy.46
  29.1 2.6 collective-permute-start
  31.7 5.6 %conditional.4 = ((f32[128,8]{0,1:T(8,128)S(1)}, f32[128,8]{0,1:T(8,128)S(1)}, f32[128,8,128]{0,2,1:T(8,128)S(1)})) conditional(s32[]{:T(128)} %convert_element_type.55, (f32[128,8]{0,1:T(8,128)S(1)}, f32[128,8]{0,1:T(8,128)S(1)}, f32[128,8,128]{0,2,1:T(8,128)S(1)}) %tuple.62, (s32[]{:T(128)}, s32[]{:T(128)}, bf16[128,576]{0,1:T(8,128)(2,1)}, ...), branch_computations={%region_1.1_spmd, %region_2.4_spmd} | conditional | flops 353913088 | bytes 8112168 | solution.py:69
  31.7 1.6 fusion.3
  33.8 1.2 fusion.29
  35.1 1.6 convolution_convert_fusion
  37.3 3.6 %collective-permute-done = bf16[128,576]{0,1:T(8,128)(2,1)S(1)} collective-permute-done((bf16[128,576]{0,1:T(8,128)(2,1)}, bf16[128,576]{0,1:T(8,128)(2,1)S(1)}, u32[]{:S(2)}, u32[]{:S(2)}) %collective-permute-start) | collective-permute-done | bytes 147488 | tf_op jit(solution)/shard_map/while/body/eval_jaxpr/ppermute | solution.py:18
  40.9 0.7 copy.46
  41.6 1.9 collective-permute-start
  43.5 5.6 %conditional.4 = ((f32[128,8]{0,1:T(8,128)S(1)}, f32[128,8]{0,1:T(8,128)S(1)}, f32[128,8,128]{0,2,1:T(8,128)S(1)})) conditional(s32[]{:T(128)} %convert_element_type.55, (f32[128,8]{0,1:T(8,128)S(1)}, f32[128,8]{0,1:T(8,128)S(1)}, f32[128,8,128]{0,2,1:T(8,128)S(1)}) %tuple.62, (s32[]{:T(128)}, s32[]{:T(128)}, bf16[128,576]{0,1:T(8,128)(2,1)}, ...), branch_computations={%region_1.1_spmd, %region_2.4_spmd} | conditional | flops 353913088 | bytes 8112168 | solution.py:69
  43.6 1.6 fusion.3
  45.6 1.2 fusion.29
  46.9 1.6 convolution_convert_fusion
  49.1 1.5 collective-permute-done
  50.7 0.7 copy.46
  51.3 1.9 collective-permute-start
  53.3 5.6 %conditional.4 = ((f32[128,8]{0,1:T(8,128)S(1)}, f32[128,8]{0,1:T(8,128)S(1)}, f32[128,8,128]{0,2,1:T(8,128)S(1)})) conditional(s32[]{:T(128)} %convert_element_type.55, (f32[128,8]{0,1:T(8,128)S(1)}, f32[128,8]{0,1:T(8,128)S(1)}, f32[128,8,128]{0,2,1:T(8,128)S(1)}) %tuple.62, (s32[]{:T(128)}, s32[]{:T(128)}, bf16[128,576]{0,1:T(8,128)(2,1)}, ...), branch_computations={%region_1.1_spmd, %region_2.4_spmd} | conditional | flops 353913088 | bytes 8112168 | solution.py:69
  53.3 1.6 fusion.3
  55.3 1.2 fusion.29
  56.7 1.6 convolution_convert_fusion
  58.8 1.5 collective-permute-done
  61.1 1.9 collective-permute-start
  63.0 10.2 %collective-permute-done = bf16[128,576]{0,1:T(8,128)(2,1)S(1)} collective-permute-done((bf16[128,576]{0,1:T(8,128)(2,1)}, bf16[128,576]{0,1:T(8,128)(2,1)S(1)}, u32[]{:S(2)}, u32[]{:S(2)}) %collective-permute-start) | collective-permute-done | bytes 147488 | tf_op jit(solution)/shard_map/while/body/eval_jaxpr/ppermute | solution.py:18
  73.3 0.7 copy.46
  73.9 1.9 collective-permute-start
  75.9 7.2 %collective-permute-done = bf16[128,576]{0,1:T(8,128)(2,1)S(1)} collective-permute-done((bf16[128,576]{0,1:T(8,128)(2,1)}, bf16[128,576]{0,1:T(8,128)(2,1)S(1)}, u32[]{:S(2)}, u32[]{:S(2)}) %collective-permute-start) | collective-permute-done | bytes 147488 | tf_op jit(solution)/shard_map/while/body/eval_jaxpr/ppermute | solution.py:18
  83.1 0.7 copy.46
  83.8 1.9 collective-permute-start
  85.7 7.2 %collective-permute-done = bf16[128,576]{0,1:T(8,128)(2,1)S(1)} collective-permute-done((bf16[128,576]{0,1:T(8,128)(2,1)}, bf16[128,576]{0,1:T(8,128)(2,1)S(1)}, u32[]{:S(2)}, u32[]{:S(2)}) %collective-permute-start) | collective-permute-done | bytes 147488 | tf_op jit(solution)/shard_map/while/body/eval_jaxpr/ppermute | solution.py:18
  93.6 2.3 collective-permute-start
  95.9 7.2 %collective-permute-done = bf16[128,576]{0,1:T(8,128)(2,1)S(1)} collective-permute-done((bf16[128,576]{0,1:T(8,128)(2,1)}, bf16[128,576]{0,1:T(8,128)(2,1)S(1)}, u32[]{:S(2)}, u32[]{:S(2)}) %collective-permute-start) | collective-permute-done | bytes 147488 | tf_op jit(solution)/shard_map/while/body/eval_jaxpr/ppermute | solution.py:18
  103.8 4.1 %collective-permute-start = (bf16[128,576]{0,1:T(8,128)(2,1)}, bf16[128,576]{0,1:T(8,128)(2,1)S(1)}, u32[]{:S(2)}, u32[]{:S(2)}) collective-permute-start(bf16[128,576]{0,1:T(8,128)(2,1)} %copy.46), channel_id=1, source_target_pairs={{0,16},{16,32},{32,48},{48,64},{64,80},{80,96},{96,112},{112,128},... | collective-permute-start | bytes 442376 | tf_op jit(solution)/shard_map/while/body/eval_jaxpr/ppermute | solution.py:18
  107.9 7.7 %collective-permute-done = bf16[128,576]{0,1:T(8,128)(2,1)S(1)} collective-permute-done((bf16[128,576]{0,1:T(8,128)(2,1)}, bf16[128,576]{0,1:T(8,128)(2,1)S(1)}, u32[]{:S(2)}, u32[]{:S(2)}) %collective-permute-start) | collective-permute-done | bytes 147488 | tf_op jit(solution)/shard_map/while/body/eval_jaxpr/ppermute | solution.py:18
  116.3 1.9 collective-permute-start
  118.2 7.1 %collective-permute-done = bf16[128,576]{0,1:T(8,128)(2,1)S(1)} collective-permute-done((bf16[128,576]{0,1:T(8,128)(2,1)}, bf16[128,576]{0,1:T(8,128)(2,1)S(1)}, u32[]{:S(2)}, u32[]{:S(2)}) %collective-permute-start) | collective-permute-done | bytes 147488 | tf_op jit(solution)/shard_map/while/body/eval_jaxpr/ppermute | solution.py:18
  125.3 0.7 copy.46
  126.0 1.9 collective-permute-start
  128.0 7.1 %collective-permute-done = bf16[128,576]{0,1:T(8,128)(2,1)S(1)} collective-permute-done((bf16[128,576]{0,1:T(8,128)(2,1)}, bf16[128,576]{0,1:T(8,128)(2,1)S(1)}, u32[]{:S(2)}, u32[]{:S(2)}) %collective-permute-start) | collective-permute-done | bytes 147488 | tf_op jit(solution)/shard_map/while/body/eval_jaxpr/ppermute | solution.py:18
  135.1 0.7 copy.46
  135.7 1.9 collective-permute-start
  137.7 7.1 %collective-permute-done = bf16[128,576]{0,1:T(8,128)(2,1)S(1)} collective-permute-done((bf16[128,576]{0,1:T(8,128)(2,1)}, bf16[128,576]{0,1:T(8,128)(2,1)S(1)}, u32[]{:S(2)}, u32[]{:S(2)}) %collective-permute-start) | collective-permute-done | bytes 147488 | tf_op jit(solution)/shard_map/while/body/eval_jaxpr/ppermute | solution.py:18
  144.8 0.7 copy.46
  145.5 1.9 collective-permute-start
  147.4 7.1 %collective-permute-done = bf16[128,576]{0,1:T(8,128)(2,1)S(1)} collective-permute-done((bf16[128,576]{0,1:T(8,128)(2,1)}, bf16[128,576]{0,1:T(8,128)(2,1)S(1)}, u32[]{:S(2)}, u32[]{:S(2)}) %collective-permute-start) | collective-permute-done | bytes 147488 | tf_op jit(solution)/shard_map/while/body/eval_jaxpr/ppermute | solution.py:18
  155.2 1.9 collective-permute-start
  157.2 7.1 %collective-permute-done = bf16[128,576]{0,1:T(8,128)(2,1)S(1)} collective-permute-done((bf16[128,576]{0,1:T(8,128)(2,1)}, bf16[128,576]{0,1:T(8,128)(2,1)S(1)}, u32[]{:S(2)}, u32[]{:S(2)}) %collective-permute-start) | collective-permute-done | bytes 147488 | tf_op jit(solution)/shard_map/while/body/eval_jaxpr/ppermute | solution.py:18
  164.4 11.4 %convolution_convert_fusion.4 = bf16[128,7168]{1,0:T(8,128)(2,1)} fusion(bf16[128,1024]{0,1:T(8,128)(2,1)S(1)} %bitcast.47, bf16[1024,7168]{0,1:T(8,128)(2,1)} %all-gather.2.cloned.1.call-done), kind=kOutput, calls=%fused_computation.49 | convolution fusion | flops 1879965696 | bytes 16777216 | tf_op jit(solution)/shard_map/dot_general | solution.py:90
  175.7 80.0 %reduce-scatter.2.cloned.1.call-done = bf16[8,7168]{1,0:T(8,128)(2,1)} async-done(((bf16[128,7168]{1,0:T(8,128)(2,1)}), bf16[8,7168]{1,0:T(8,128)(2,1)}) %reduce-scatter.2.cloned.1.call-update) | async-done | bytes 114704 | tf_op jit(solution)/shard_map/reduce_scatter | solution.py:95
  (73 shorter events, 8.8 us)
Async XLA Ops:
  6.5 157.8 %all-gather.2.cloned.1.call-start = ((), (), s32[]{:S(2)}) async-start(), calls=%async_computation.1 | async-start | bytes 15597568 | tf_op jit(solution)/shard_map/all_gather | solution.py:92
  7.5 248.3 %reduce-scatter.2.cloned.1.call-start = ((), (), s32[]{:S(2)}) async-start(), calls=%async_computation.2 | async-start | bytes 1949696 | tf_op jit(solution)/shard_map/reduce_scatter | solution.py:95
  8.6 155.7 %copy-start = (bf16[128,8,128]{2,1,0:T(8,128)(2,1)S(1)}, bf16[128,8,128]{2,1,0:T(8,128)(2,1)}, u32[]{:S(2)}) copy-start(bf16[128,8,128]{2,1,0:T(8,128)(2,1)} %param.12) | copy-start | bytes 786436
  9.3 9.1 %collective-permute-start = (bf16[128,576]{0,1:T(8,128)(2,1)}, bf16[128,576]{0,1:T(8,128)(2,1)S(1)}, u32[]{:S(2)}, u32[]{:S(2)}) collective-permute-start(bf16[128,576]{0,1:T(8,128)(2,1)} %copy.46), channel_id=1, source_target_pairs={{0,16},{16,32},{32,48},{48,64},{64,80},{80,96},{96,112},{112,128},... | collective-permute-start | bytes 442376 | tf_op jit(solution)/shard_map/while/body/eval_jaxpr/ppermute | solution.py:18
  19.0 9.4 %collective-permute-start = (bf16[128,576]{0,1:T(8,128)(2,1)}, bf16[128,576]{0,1:T(8,128)(2,1)S(1)}, u32[]{:S(2)}, u32[]{:S(2)}) collective-permute-start(bf16[128,576]{0,1:T(8,128)(2,1)} %copy.46), channel_id=1, source_target_pairs={{0,16},{16,32},{32,48},{48,64},{64,80},{80,96},{96,112},{112,128},... | collective-permute-start | bytes 442376 | tf_op jit(solution)/shard_map/while/body/eval_jaxpr/ppermute | solution.py:18
  29.1 11.8 %collective-permute-start = (bf16[128,576]{0,1:T(8,128)(2,1)}, bf16[128,576]{0,1:T(8,128)(2,1)S(1)}, u32[]{:S(2)}, u32[]{:S(2)}) collective-permute-start(bf16[128,576]{0,1:T(8,128)(2,1)} %copy.46), channel_id=1, source_target_pairs={{0,16},{16,32},{32,48},{48,64},{64,80},{80,96},{96,112},{112,128},... | collective-permute-start | bytes 442376 | tf_op jit(solution)/shard_map/while/body/eval_jaxpr/ppermute | solution.py:18
  41.6 9.1 %collective-permute-start = (bf16[128,576]{0,1:T(8,128)(2,1)}, bf16[128,576]{0,1:T(8,128)(2,1)S(1)}, u32[]{:S(2)}, u32[]{:S(2)}) collective-permute-start(bf16[128,576]{0,1:T(8,128)(2,1)} %copy.46), channel_id=1, source_target_pairs={{0,16},{16,32},{32,48},{48,64},{64,80},{80,96},{96,112},{112,128},... | collective-permute-start | bytes 442376 | tf_op jit(solution)/shard_map/while/body/eval_jaxpr/ppermute | solution.py:18
  51.3 9.1 %collective-permute-start = (bf16[128,576]{0,1:T(8,128)(2,1)}, bf16[128,576]{0,1:T(8,128)(2,1)S(1)}, u32[]{:S(2)}, u32[]{:S(2)}) collective-permute-start(bf16[128,576]{0,1:T(8,128)(2,1)} %copy.46), channel_id=1, source_target_pairs={{0,16},{16,32},{32,48},{48,64},{64,80},{80,96},{96,112},{112,128},... | collective-permute-start | bytes 442376 | tf_op jit(solution)/shard_map/while/body/eval_jaxpr/ppermute | solution.py:18
  61.1 12.2 %collective-permute-start = (bf16[128,576]{0,1:T(8,128)(2,1)}, bf16[128,576]{0,1:T(8,128)(2,1)S(1)}, u32[]{:S(2)}, u32[]{:S(2)}) collective-permute-start(bf16[128,576]{0,1:T(8,128)(2,1)} %copy.46), channel_id=1, source_target_pairs={{0,16},{16,32},{32,48},{48,64},{64,80},{80,96},{96,112},{112,128},... | collective-permute-start | bytes 442376 | tf_op jit(solution)/shard_map/while/body/eval_jaxpr/ppermute | solution.py:18
  73.9 9.2 %collective-permute-start = (bf16[128,576]{0,1:T(8,128)(2,1)}, bf16[128,576]{0,1:T(8,128)(2,1)S(1)}, u32[]{:S(2)}, u32[]{:S(2)}) collective-permute-start(bf16[128,576]{0,1:T(8,128)(2,1)} %copy.46), channel_id=1, source_target_pairs={{0,16},{16,32},{32,48},{48,64},{64,80},{80,96},{96,112},{112,128},... | collective-permute-start | bytes 442376 | tf_op jit(solution)/shard_map/while/body/eval_jaxpr/ppermute | solution.py:18
  83.8 9.2 %collective-permute-start = (bf16[128,576]{0,1:T(8,128)(2,1)}, bf16[128,576]{0,1:T(8,128)(2,1)S(1)}, u32[]{:S(2)}, u32[]{:S(2)}) collective-permute-start(bf16[128,576]{0,1:T(8,128)(2,1)} %copy.46), channel_id=1, source_target_pairs={{0,16},{16,32},{32,48},{48,64},{64,80},{80,96},{96,112},{112,128},... | collective-permute-start | bytes 442376 | tf_op jit(solution)/shard_map/while/body/eval_jaxpr/ppermute | solution.py:18
  93.6 9.5 %collective-permute-start = (bf16[128,576]{0,1:T(8,128)(2,1)}, bf16[128,576]{0,1:T(8,128)(2,1)S(1)}, u32[]{:S(2)}, u32[]{:S(2)}) collective-permute-start(bf16[128,576]{0,1:T(8,128)(2,1)} %copy.46), channel_id=1, source_target_pairs={{0,16},{16,32},{32,48},{48,64},{64,80},{80,96},{96,112},{112,128},... | collective-permute-start | bytes 442376 | tf_op jit(solution)/shard_map/while/body/eval_jaxpr/ppermute | solution.py:18
  103.8 11.8 %collective-permute-start = (bf16[128,576]{0,1:T(8,128)(2,1)}, bf16[128,576]{0,1:T(8,128)(2,1)S(1)}, u32[]{:S(2)}, u32[]{:S(2)}) collective-permute-start(bf16[128,576]{0,1:T(8,128)(2,1)} %copy.46), channel_id=1, source_target_pairs={{0,16},{16,32},{32,48},{48,64},{64,80},{80,96},{96,112},{112,128},... | collective-permute-start | bytes 442376 | tf_op jit(solution)/shard_map/while/body/eval_jaxpr/ppermute | solution.py:18
  116.3 9.1 %collective-permute-start = (bf16[128,576]{0,1:T(8,128)(2,1)}, bf16[128,576]{0,1:T(8,128)(2,1)S(1)}, u32[]{:S(2)}, u32[]{:S(2)}) collective-permute-start(bf16[128,576]{0,1:T(8,128)(2,1)} %copy.46), channel_id=1, source_target_pairs={{0,16},{16,32},{32,48},{48,64},{64,80},{80,96},{96,112},{112,128},... | collective-permute-start | bytes 442376 | tf_op jit(solution)/shard_map/while/body/eval_jaxpr/ppermute | solution.py:18
  126.0 9.1 %collective-permute-start = (bf16[128,576]{0,1:T(8,128)(2,1)}, bf16[128,576]{0,1:T(8,128)(2,1)S(1)}, u32[]{:S(2)}, u32[]{:S(2)}) collective-permute-start(bf16[128,576]{0,1:T(8,128)(2,1)} %copy.46), channel_id=1, source_target_pairs={{0,16},{16,32},{32,48},{48,64},{64,80},{80,96},{96,112},{112,128},... | collective-permute-start | bytes 442376 | tf_op jit(solution)/shard_map/while/body/eval_jaxpr/ppermute | solution.py:18
  135.7 9.1 %collective-permute-start = (bf16[128,576]{0,1:T(8,128)(2,1)}, bf16[128,576]{0,1:T(8,128)(2,1)S(1)}, u32[]{:S(2)}, u32[]{:S(2)}) collective-permute-start(bf16[128,576]{0,1:T(8,128)(2,1)} %copy.46), channel_id=1, source_target_pairs={{0,16},{16,32},{32,48},{48,64},{64,80},{80,96},{96,112},{112,128},... | collective-permute-start | bytes 442376 | tf_op jit(solution)/shard_map/while/body/eval_jaxpr/ppermute | solution.py:18
  145.5 9.1 %collective-permute-start = (bf16[128,576]{0,1:T(8,128)(2,1)}, bf16[128,576]{0,1:T(8,128)(2,1)S(1)}, u32[]{:S(2)}, u32[]{:S(2)}) collective-permute-start(bf16[128,576]{0,1:T(8,128)(2,1)} %copy.46), channel_id=1, source_target_pairs={{0,16},{16,32},{32,48},{48,64},{64,80},{80,96},{96,112},{112,128},... | collective-permute-start | bytes 442376 | tf_op jit(solution)/shard_map/while/body/eval_jaxpr/ppermute | solution.py:18
  155.2 9.1 %collective-permute-start = (bf16[128,576]{0,1:T(8,128)(2,1)}, bf16[128,576]{0,1:T(8,128)(2,1)S(1)}, u32[]{:S(2)}, u32[]{:S(2)}) collective-permute-start(bf16[128,576]{0,1:T(8,128)(2,1)} %copy.46), channel_id=1, source_target_pairs={{0,16},{16,32},{32,48},{48,64},{64,80},{80,96},{96,112},{112,128},... | collective-permute-start | bytes 442376 | tf_op jit(solution)/shard_map/while/body/eval_jaxpr/ppermute | solution.py:18
Sparse Core Ops, SparseCore 0:
  10.1 115.2 all-gather.1
  175.9 79.8 reduce-scatter.1
where the time goes:
time: 264 us; the launch traced here: 263 us
  waiting for transfers between devices  163 us (62%)
  matrix products  37 us (14%)
  starting transfers between devices  33.7 us (13%)
  between operations  13.5 us (5%)
  local copies, waits for them, and re-layouts  12.8 us (5%)
    ppermute x15, waiting for transfers between devices, shifted(): return lax.ppermute(shard, axis, pairs)  83.2 us
    reduce_scatter x1, waiting for transfers between devices, local(): lax.psum_scatter(partial_sum.astype(jnp.bfloat16), 'head', scatter_dimens...  80 us
    ppermute x15, starting transfers between devices, shifted(): return lax.ppermute(shard, axis, pairs)  33.6 us
    dot_general x1, matrix products, local(): jnp.dot(attention, lax.all_gather(out_proj, 'ctx', axis=1, tiled=True), p...  11.4 us
    another operation x15, local copies, waits for them, and re-layouts  10 us
    dot_general x5, matrix products, attend(): jnp.dot(latent, value_up, preferred_element_type=jnp.float32)  8.23 us
    dot_general x5, matrix products, attend(): jnp.dot(latent, key_up, preferred_element_type=jnp.float32)  8.19 us
    dot_general x5, matrix products, attend(): jnp.einsum('qhr,kr->qhk', query_rope, rope_keys, preferred_element_type=j...  5.98 us
  transfers between devices with their start and end apart: 17, of which 15 were waited for; matrix products, arithmetic and copies ran while one was open for 15% of the time, Pallas kernels for 0%

commit v1 on v0

v1 whole, which is shorter than its diff:
```python
import functools

import jax
import jax.numpy as jnp
from jax import lax
from jax.experimental import pallas as pl
from jax.experimental.pallas import tpu as pltpu
from jax.sharding import PartitionSpec as P

LAT = 512
ROPE = 64
NOPE = 128
VD = 128
HEADS = 8
BLOCK = 128
COLS = 448
MASKED = -1e30
LOG2E = 1.4426950408889634
MESH = pl.DeviceIdType.MESH
BF16 = jnp.bfloat16
F32 = jnp.float32


def dot(a, b, contract):
    return lax.dot_general(a, b, ((contract[0], contract[1]), ((), ())), preferred_element_type=F32)


def kernel(
    q_hbm, qrt_hbm, latt_hbm, ku_hbm, vu_hbm, wt_hbm, out_ref,
    q_v, qrt_v, ku_v, vu_v, wt, qf, qa, qr, lt, kvr, kvt, m_s, l_s, acc, att,
    part, direct, sbuf, rbuf, dbuf, fin, landed,
    loc_sem, w_sem, p1_send, p1_recv, p3_send, p3_recv, swap_send, swap_recv,
    rs_send, rs_recv, d_send, d_recv, a_send, a_recv,
):
    c = lax.axis_index("ctx")
    h = lax.axis_index("head")
    x, yh, k = c // 4, (c // 2) % 2, c % 2
    z, yl = h // 2, h % 2

    def place(dx, flip=False):
        return ((x + dx) % 4) * 2 + ((1 - yh) if flip else yh)

    here = place(0)
    local = [
        pltpu.make_async_copy(src, dst, loc_sem.at[i])
        for i, (src, dst) in enumerate(
            [(latt_hbm, lt.at[here, k]), (q_hbm, q_v), (ku_hbm, ku_v), (qrt_hbm, qrt_v), (vu_hbm, vu_v), (wt_hbm, wt.at[yl])]
        )
    ]
    for copy in local:
        copy.start()

    core = (here * 2 + 1 - k, h)
    xp = (place(1) * 2 + k, h)
    xm = (place(3) * 2 + k, h)
    y_far = (place(0, True) * 2 + k, h)
    y_near = (place(0, True) * 2 + k, z * 2 + 1 - yl)
    y_low = (c, z * 2 + 1 - yl)
    y_cross = (here * 2 + 1 - k, z * 2 + 1 - yl)
    zp = (c, ((z + 1) % 8) * 2 + yl)
    zm = (c, ((z + 7) % 8) * 2 + yl)

    barrier = pltpu.get_barrier_semaphore()
    greeted = [((c + i) % 16, h) for i in range(1, 16)]
    greeted += [((c + i) % 16, z * 2 + 1 - yl) for i in range(16)]
    greeted += [(c, ((z + i) % 8) * 2 + yl) for i in range(1, 8)]
    for peer in greeted:
        pl.semaphore_signal(barrier, inc=1, device_id=peer, device_id_type=MESH)

    local[1].wait()
    local[2].wait()
    qf[...] = q_v[...].astype(F32).reshape(BLOCK * HEADS, NOPE)
    for i in range(HEADS):
        q_head = qf[pl.ds(i, BLOCK, stride=HEADS), :].astype(BF16)
        absorbed = dot(q_head, ku_v[:, i * NOPE : (i + 1) * NOPE], ((1,), (1,)))
        qa[i * BLOCK : (i + 1) * BLOCK] = absorbed.astype(BF16)
    local[3].wait()
    for i in range(HEADS):
        qr[i // 2, :, (i % 2) * BLOCK : (i % 2 + 1) * BLOCK] = qrt_v[i]
    local[0].wait()
    local[5].wait()

    pl.semaphore_wait(barrier, len(greeted))

    def gather(at, size, send, recv, y_peer):
        LO, HI, ALL = (0, size // 2), (size // 2, size // 2), (0, size)
        table = [
            (place(0), LO, y_peer, place(0, True)),
            (place(0), HI, y_peer, place(0, True)),
            (place(0), LO, xp, place(3)),
            (place(0), HI, xp, place(3)),
            (place(0), HI, xm, place(1)),
            (place(0), LO, xm, place(1)),
            (place(0, True), LO, xp, place(3, True)),
            (place(0, True), HI, xp, place(3, True)),
            (place(0, True), HI, xm, place(1, True)),
            (place(0, True), LO, xm, place(1, True)),
            (place(3), LO, xp, place(2)),
            (place(1), HI, xm, place(2)),
            (place(3, True), LO, xp, place(2, True)),
            (place(1, True), HI, xm, place(2, True)),
        ]
        table += [(spot, ALL, core, spot) for spot in (place(0), place(0, True), place(3), place(1), place(3, True), place(1, True), place(2), place(2, True))]

        def copy(e, index):
            _, rows, peer, _ = table[e]
            slot = (1 - k) if e >= 14 and index == 3 else k
            ref = at(table[e][index], slot, rows)
            return pltpu.make_async_remote_copy(
                src_ref=ref, dst_ref=ref, send_sem=send.at[e], recv_sem=recv.at[e],
                device_id=peer, device_id_type=MESH,
            )

        def start(*events):
            for e in events:
                copy(e, 0).start()

        def arrive(*events):
            for e in events:
                copy(e, 3).wait_recv()

        def drain():
            for e in range(len(table)):
                copy(e, 0).wait_send()

        return start, arrive, drain

    start1, arrive1, drain1 = gather(
        lambda i, s, rows: lt.at[i, s, pl.ds(rows[0], rows[1])], LAT + ROPE, p1_send, p1_recv, y_near
    )
    start3, arrive3, drain3 = gather(
        lambda i, s, rows: att.at[i, s, pl.ds(rows[0], rows[1])], BLOCK, p3_send, p3_recv, y_far
    )

    start1(2, 4, 0, 3, 5, 1, 14)
    w_copy = pltpu.make_async_remote_copy(
        src_ref=wt.at[yl], dst_ref=wt.at[yl], send_sem=w_sem.at[0], recv_sem=w_sem.at[1],
        device_id=y_low, device_id_type=MESH,
    )
    w_copy.start()

    def attend(group, diagonal):
        for b in range(4):
            tile = lt[group * 2 + b // 2, b % 2]
            kvt[:, b * BLOCK : (b + 1) * BLOCK] = tile[:LAT]
            kvr[b * BLOCK : (b + 1) * BLOCK] = tile.T

        def heads(i, _):
            rows = pl.ds(pl.multiple_of(i * 256, 256), 256)
            scores = dot(kvr[:, :LAT], qa[rows], ((1,), (1,)))
            scores += dot(kvr[:, LAT:], qr[i], ((1,), (0,)))
            scores = scores * ((NOPE + ROPE) ** -0.5 * LOG2E)
            if diagonal:
                key_pos = group * 512 + lax.broadcasted_iota(jnp.int32, (512, 256), 0)
                query_pos = c * BLOCK + lax.broadcasted_iota(jnp.int32, (512, 256), 1) % BLOCK
                scores = jnp.where(key_pos <= query_pos, scores, MASKED)
                new_max = jnp.max(scores, axis=0, keepdims=True)
                exps = jnp.exp2(scores - new_max)
                l_s[i] = jnp.sum(exps, axis=0, keepdims=True)
                acc[i] = dot(kvt[...], exps.astype(BF16), ((1,), (0,)))
            else:
                new_max = jnp.maximum(m_s[i], jnp.max(scores, axis=0, keepdims=True))
                rescale = jnp.exp2(m_s[i] - new_max)
                exps = jnp.exp2(scores - new_max)
                l_s[i] = l_s[i] * rescale + jnp.sum(exps, axis=0, keepdims=True)
                acc[i] = acc[i] * rescale + dot(kvt[...], exps.astype(BF16), ((1,), (0,)))
            m_s[i] = new_max
            return 0

        lax.fori_loop(0, 4, heads, 0)

    arrive1(2)
    start1(10)
    arrive1(4)
    start1(11)
    arrive1(0)
    start1(6, 9)
    arrive1(1)
    start1(8, 7, 15)
    arrive1(3, 5)
    start1(16, 17)
    arrive1(14, 15)
    attend(x, True)
    arrive1(6)
    start1(12)
    arrive1(8)
    start1(13)
    arrive1(7, 9)
    start1(18, 19)
    arrive1(10, 11)
    start1(20)
    arrive1(16, 18)

    @pl.when(x >= 1)
    def _():
        attend(x - 1, False)

    arrive1(12, 13)
    start1(21)
    arrive1(17, 19)

    @pl.when(x == 3)
    def _():
        attend(0, False)

    arrive1(20, 21)

    @pl.when(x >= 2)
    def _():
        attend(x - 2, False)

    local[4].wait()
    mine = jnp.where(k == yl, here, 8)
    for i in range(HEADS // 2):
        normed = (acc[i] / l_s[i]).T.astype(BF16)
        for j in range(2):
            cols = slice((2 * i + j) * VD, (2 * i + j + 1) * VD)
            att[mine, k, :, cols] = dot(
                normed[j * BLOCK : (j + 1) * BLOCK], vu_v[:, cols], ((1,), (0,))
            ).astype(BF16)

    def swap(half, outgoing):
        rows = pl.ds(half * 64, 64)
        return pltpu.make_async_remote_copy(
            src_ref=att.at[8, k, rows], dst_ref=att.at[here, (1 - k) if outgoing else k, rows],
            send_sem=swap_send.at[half], recv_sem=swap_recv.at[half], device_id=y_cross, device_id_type=MESH,
        )

    @pl.when(k == yl)
    def _():
        start3(2, 4, 0, 3, 5, 1, 14)

    @pl.when(k != yl)
    def _():
        swap(0, True).start()
        swap(1, True).start()
        swap(0, False).wait_recv()
        start3(2, 0)
        swap(1, False).wait_recv()
        start3(4, 1, 3, 5, 14)

    def spots(r):
        return ((place(0), place(0, True)), (place(3), place(1)), (place(3, True), place(1, True)), (place(2), place(2, True)))[r]

    def project(r, slot):
        spot = spots(r)[slot]
        product = dot(att[spot, 0], wt[0], ((1,), (1,))) + dot(att[spot, 1], wt[1], ((1,), (1,)))
        for zd in range(8):
            piece = product[zd * 16 : zd * 16 + 16]
            part[r, zd, slot * 16 : slot * 16 + 16] = piece
            if r >= 2:
                direct[r - 2, zd, slot * 16 : slot * 16 + 16] = piece.astype(BF16)

    def rs_copy(r, t, d):
        e = r * 8 + t * 2 + d
        rows = pl.ds(0, 32) if t else pl.ds(16 * d, 16)
        return pltpu.make_async_remote_copy(
            src_ref=sbuf.at[e, rows], dst_ref=rbuf.at[e, rows], send_sem=rs_send.at[e],
            recv_sem=rs_recv.at[e], device_id=(zp, zm)[d], device_id_type=MESH,
        )

    def rs_step(r, t):
        for d in range(2):
            e = r * 8 + t * 2 + d
            dest = (z + 4 - t) % 8 if d == 0 else (z + 4 + t) % 8
            if t == 0:
                rows = pl.ds(16 * d, 16)
                sbuf[e, rows] = part[r, dest, rows].astype(BF16)
            else:
                rs_copy(r, t - 1, d).wait_recv()
                if t == 1:
                    add, own = pl.ds(16 * d, 16), pl.ds(16 - 16 * d, 16)
                    sbuf[e, add] = (part[r, dest, add] + rbuf[e - 2, add].astype(F32)).astype(BF16)
                    sbuf[e, own] = part[r, dest, own].astype(BF16)
                else:
                    sbuf[e] = (part[r, dest] + rbuf[e - 2].astype(F32)).astype(BF16)
            rs_copy(r, t, d).start()

    def d_copy(r, i):
        return pltpu.make_async_remote_copy(
            src_ref=direct.at[r - 2, (z + i) % 8], dst_ref=dbuf.at[r - 2, i - 1], send_sem=d_send.at[r - 2, i - 1],
            recv_sem=d_recv.at[r - 2, i - 1], device_id=(c, ((z + i) % 8) * 2 + yl), device_id_type=MESH,
        )

    def a_copy(r, slot, y2):
        e = r * 4 + slot * 2 + y2
        at = slot * 16 + y2 * 8
        return pltpu.make_async_remote_copy(
            src_ref=fin.at[r, pl.ds(at, 8)], dst_ref=landed.at[c], send_sem=a_send.at[e],
            recv_sem=a_recv.at[c], device_id=(spots(r)[slot] * 2 + yl, z * 2 + y2), device_id_type=MESH,
        )

    def finish(r):
        if r < 2:
            rs_copy(r, 3, 0).wait_recv()
            rs_copy(r, 3, 1).wait_recv()
            fin[r] = part[r, z] + rbuf[r * 8 + 6].astype(F32) + rbuf[r * 8 + 7].astype(F32)
        else:
            total = part[r, z]
            for i in range(1, 8):
                d_copy(r, i).wait_recv()
                total = total + dbuf[r - 2, i - 1].astype(F32)
            fin[r] = total
        for slot in range(2):
            for y2 in range(2):
                if r == 0 and slot == 0:
                    self_copy = (k == yl) & (yl == y2)

                    @pl.when(jnp.logical_not(self_copy))
                    def _():
                        a_copy(r, slot, y2).start()

                    @pl.when(self_copy)
                    def _():
                        landed[c] = fin[r, y2 * 8 : y2 * 8 + 8]
                else:
                    a_copy(r, slot, y2).start()

    arrive3(2)
    start3(10)
    arrive3(4)
    start3(11)
    arrive3(0)
    start3(6, 9)
    arrive3(1)
    start3(8, 7, 15)
    arrive3(3, 5)
    start3(16, 17)
    w_copy.wait_recv()
    arrive3(14)
    project(0, 0)
    arrive3(15)
    project(0, 1)
    rs_step(0, 0)
    arrive3(16, 17)
    project(1, 0)
    project(1, 1)
    rs_step(1, 0)
    arrive3(10, 11)
    start3(20)
    rs_step(0, 1)
    arrive3(6)
    start3(12)
    arrive3(8)
    start3(13)
    rs_step(1, 1)
    rs_step(0, 2)
    arrive3(7, 9)
    start3(18, 19)
    rs_step(1, 2)
    arrive3(18, 19)
    project(2, 0)
    project(2, 1)
    for i in range(1, 8):
        d_copy(2, i).start()
    arrive3(20)
    project(3, 0)
    rs_step(0, 3)
    rs_step(1, 3)
    arrive3(12, 13)
    start3(21)
    arrive3(21)
    project(3, 1)
    for i in range(1, 8):
        d_copy(3, i).start()
    for r in range(4):
        finish(r)

    for c2 in range(16):

        @pl.when(jnp.logical_or(c != c2, yl != k))
        def _():
            pltpu.make_async_remote_copy(
                src_ref=landed.at[c2], dst_ref=landed.at[c2], send_sem=a_send.at[c2],
                recv_sem=a_recv.at[c2], device_id=core, device_id_type=MESH,
            ).wait_recv()

    out_ref[...] = jnp.concatenate([landed[c2] for c2 in range(16)], axis=1).astype(BF16)

    drain1()
    drain3()
    w_copy.wait_send()

    @pl.when(k != yl)
    def _():
        swap(0, True).wait_send()
        swap(1, True).wait_send()

    for r in range(4):
        if r < 2:
            for t in range(4):
                for d in range(2):
                    rs_copy(r, t, d).wait_send()
        else:
            for i in range(1, 8):
                d_copy(r, i).wait_send()
        for slot in range(2):
            for y2 in range(2):

                @pl.when(jnp.logical_not((k == yl) & (yl == y2) & (r == 0) & (slot == 0)))
                def _():
                    a_copy(r, slot, y2).wait_send()


def local(queries, query_rope, latent_cache, key_up, value_up, out_proj):
    dma = pltpu.SemaphoreType.DMA
    return pl.pallas_call(
        kernel,
        out_shape=jax.ShapeDtypeStruct((8, 7168), BF16),
        in_specs=[pl.BlockSpec(memory_space=pl.ANY)] * 6,
        out_specs=pl.BlockSpec(memory_space=pltpu.VMEM),
        scratch_shapes=[
            pltpu.VMEM((BLOCK, HEADS, NOPE), BF16),
            pltpu.VMEM((HEADS, ROPE, BLOCK), BF16),
            pltpu.VMEM((LAT, HEADS * NOPE), BF16),
            pltpu.VMEM((LAT, HEADS * VD), BF16),
            pltpu.VMEM((2, COLS, HEADS * VD), BF16),
            pltpu.VMEM((BLOCK * HEADS, NOPE), F32),
            pltpu.VMEM((BLOCK * HEADS, LAT), BF16),
            pltpu.VMEM((HEADS // 2, ROPE, 2 * BLOCK), BF16),
            pltpu.VMEM((8, 2, LAT + ROPE, BLOCK), BF16),
            pltpu.VMEM((512, LAT + ROPE), BF16),
            pltpu.VMEM((LAT, 512), BF16),
            pltpu.VMEM((4, 1, 256), F32),
            pltpu.VMEM((4, 1, 256), F32),
            pltpu.VMEM((4, LAT, 256), F32),
            pltpu.VMEM((9, 2, BLOCK, HEADS * VD), BF16),
            pltpu.VMEM((4, 8, 32, COLS), F32),
            pltpu.VMEM((2, 8, 32, COLS), BF16),
            pltpu.VMEM((16, 32, COLS), BF16),
            pltpu.VMEM((16, 32, COLS), BF16),
            pltpu.VMEM((2, 7, 32, COLS), BF16),
            pltpu.VMEM((4, 32, COLS), F32),
            pltpu.VMEM((16, 8, COLS), F32),
            dma((6,)), dma((2,)), dma((22,)), dma((22,)), dma((22,)), dma((22,)), dma((2,)), dma((2,)),
            dma((16,)), dma((16,)), dma((2, 7)), dma((2, 7)), dma((16,)), dma((16,)),
        ],
        compiler_params=pltpu.CompilerParams(
            collective_id=0, has_side_effects=True, vmem_limit_bytes=63 * 1024 * 1024
        ),
    )(queries, query_rope.transpose(1, 2, 0), latent_cache.T, key_up, value_up, out_proj.T)


def solution(mesh):
    placed = (
        P("ctx", "head", None),
        P("ctx", "head", None),
        P("ctx", None),
        P(None, "head"),
        P(None, "head"),
        P("head", "ctx"),
    )
    return jax.shard_map(
        local, mesh=mesh, in_specs=placed, out_specs=P(("ctx", "head"), None), check_vma=False
    )
```

time: 264 us -> 84.2 us (0.32)
  the two profiles are of different devices: /device:TPU:2 before, /device:TPU:1 now
where the time goes in v1:
time: 84.2 us; the launch traced here: 84.1 us
  Pallas kernels  82.5 us (98%)
  local copies, waits for them, and re-layouts  1.55 us (2%)
    pallas_call x1, Pallas kernels, local(): pl.pallas_call(kernel, out_shape=jax.ShapeDtypeStruct((8, 7168), BF16), i...  82.5 us

profile of v1, /device:TPU:1, one launch (start us, length us, event | category | flops | bytes accessed | tf_op | source)
XLA Modules:
  0.0 84.1 jit_solution(7120292554820141170)
XLA Ops:
  0.0 82.5 %shard_map.64 = bf16[8,7168]{1,0:T(8,128)(2,1)} custom-call(bf16[128,8,128]{2,1,0:T(8,128)(2,1)} %q_hbm.1, bf16[8,64,128]{2,1,0:T(8,128)(2,1)} %bitcast.5, bf16[576,128]{1,0:T(8,128)(2,1)} %bitcast.4, bf16[512,1024]{1,0:T(8,128)(2,1)} %ku_hbm.1, bf16[512,1024]{1,0:T(8,128)(2,1)} %vu_hbm.1, bf16[448,1024]{1,0:T(8,128)(2,1)} %bitcast.3), custom_call_target="tpu_custom_call" | custom-call | tf_op jit(solution)/shard_map/pallas_call | solution.py:407
  82.5 1.6 %copy.8 = bf16[8,7168]{1,0:T(8,128)(2,1)} copy(bf16[8,7168]{1,0:T(8,128)(2,1)} %shard_map.64) | data formatting | bytes 229376

commit v2 on v1

v2 whole, which is shorter than its diff:
```python
import functools

import jax
import jax.numpy as jnp
from jax import lax
from jax.experimental import pallas as pl
from jax.experimental.pallas import tpu as pltpu
from jax.sharding import PartitionSpec as P

LAT = 512
ROPE = 64
NOPE = 128
VD = 128
HEADS = 8
BLOCK = 128
COLS = 448
MASKED = -1e30
LOG2E = 1.4426950408889634
MESH = pl.DeviceIdType.MESH
BF16 = jnp.bfloat16
F32 = jnp.float32


def dot(a, b, contract):
    return lax.dot_general(a, b, ((contract[0], contract[1]), ((), ())), preferred_element_type=F32)


def kernel(
    q_hbm, qrt_hbm, latt_hbm, ku_hbm, vu_hbm, wt_hbm, out_ref,
    q_v, qrt_v, ku_v, vu_v, wt, qf, qa, lt, m_s, l_s, acc, att,
    part, direct, sbuf, rbuf, dbuf, fin, landed,
    loc_sem, w_sem, p1_send, p1_recv, p3_send, p3_recv, swap_send, swap_recv,
    rs_send, rs_recv, d_send, d_recv, a_send, a_recv,
):
    c = lax.axis_index("ctx")
    h = lax.axis_index("head")
    x, yh, k = c // 4, (c // 2) % 2, c % 2
    z, yl = h // 2, h % 2

    def place(dx, flip=False):
        return ((x + dx) % 4) * 2 + ((1 - yh) if flip else yh)

    here = place(0)
    local = [
        pltpu.make_async_copy(src, dst, loc_sem.at[i])
        for i, (src, dst) in enumerate(
            [(latt_hbm, lt.at[here, k]), (q_hbm, q_v), (ku_hbm, ku_v), (qrt_hbm, qrt_v), (vu_hbm, vu_v), (wt_hbm, wt.at[yl])]
        )
    ]
    for copy in local:
        copy.start()

    core = (here * 2 + 1 - k, h)
    xp = (place(1) * 2 + k, h)
    xm = (place(3) * 2 + k, h)
    y_far = (place(0, True) * 2 + k, h)
    y_near = (place(0, True) * 2 + k, z * 2 + 1 - yl)
    y_low = (c, z * 2 + 1 - yl)
    y_cross = (here * 2 + 1 - k, z * 2 + 1 - yl)
    y_near_cross = (place(0, True) * 2 + 1 - k, z * 2 + 1 - yl)
    zp = (c, ((z + 1) % 8) * 2 + yl)
    zm = (c, ((z + 7) % 8) * 2 + yl)

    barrier = pltpu.get_barrier_semaphore()
    greeted = [((c + i) % 16, h) for i in range(1, 16)]
    greeted += [((c + i) % 16, z * 2 + 1 - yl) for i in range(16)]
    greeted += [(c, ((z + i) % 8) * 2 + yl) for i in range(1, 8)]
    for peer in greeted:
        pl.semaphore_signal(barrier, inc=1, device_id=peer, device_id_type=MESH)

    local[1].wait()
    local[2].wait()
    qf[...] = q_v[...].astype(F32).reshape(BLOCK * HEADS, NOPE)
    for i in range(HEADS):
        q_head = qf[pl.ds(i, BLOCK, stride=HEADS), :].astype(BF16)
        absorbed = dot(q_head, ku_v[:, i * NOPE : (i + 1) * NOPE], ((1,), (1,)))
        qa[i * BLOCK : (i + 1) * BLOCK, :LAT] = absorbed.astype(BF16)
    local[3].wait()
    for i in range(HEADS):
        qa[i * BLOCK : (i + 1) * BLOCK, LAT:] = qrt_v[i].T
    local[0].wait()
    local[5].wait()

    pl.semaphore_wait(barrier, len(greeted))

    def gather(at, send, recv, y_peer, last):
        LO, HI, ALL = 0, 1, None
        table = [
            (place(0), LO, y_peer, place(0, True)),
            (place(0), HI, y_peer, place(0, True)),
            (place(0), LO, xp, place(3)),
            (place(0), HI, xp, place(3)),
            (place(0), HI, xm, place(1)),
            (place(0), LO, xm, place(1)),
            (place(0, True), LO, xp, place(3, True)),
            (place(0, True), HI, xp, place(3, True)),
            (place(0, True), HI, xm, place(1, True)),
            (place(0, True), LO, xm, place(1, True)),
            (place(3), LO, xp, place(2)),
            (place(1), HI, xm, place(2)),
        ] + last
        table += [(spot, ALL, core, spot) for spot in (place(0), place(0, True), place(3), place(1), place(3, True), place(1, True), place(2), place(2, True))]

        def copy(e, index):
            _, part_of, peer, _ = table[e]
            slot = (1 - k) if e >= 14 and index == 3 else k
            ref = at(table[e][index], slot, part_of)
            return pltpu.make_async_remote_copy(
                src_ref=ref, dst_ref=ref, send_sem=send.at[e], recv_sem=recv.at[e],
                device_id=peer, device_id_type=MESH,
            )

        def start(*events):
            for e in events:
                copy(e, 0).start()

        def arrive(*events):
            for e in events:
                copy(e, 3).wait_recv()

        def drain():
            for e in range(len(table)):
                copy(e, 0).wait_send()

        return start, arrive, drain

    def latent_at(i, s, half):
        return lt.at[i, s] if half is None else lt.at[i, s, pl.ds(half * 288, 288)]

    def att_at(i, s, half):
        return att.at[i, s] if half is None else att.at[i, s, half]

    by_x = [(place(3, True), 0, xp, place(2, True)), (place(1, True), 1, xm, place(2, True))]
    by_y = [(place(2), 0, y_far, place(2, True)), (place(2), 1, y_far, place(2, True))]
    start1, arrive1, drain1 = gather(latent_at, p1_send, p1_recv, y_near, by_x)
    start3, arrive3, drain3 = gather(att_at, p3_send, p3_recv, y_far, by_x)

    start1(2, 4, 0, 3, 5, 1, 14)

    def w_copy(i):
        rows = (pl.ds(0, 384), pl.ds(384, 64))[i]
        return pltpu.make_async_remote_copy(
            src_ref=wt.at[yl, rows], dst_ref=wt.at[yl, rows], send_sem=w_sem.at[i], recv_sem=w_sem.at[2 + i],
            device_id=y_low, device_id_type=MESH,
        )

    w_copy(0).start()

    def attend(spot, diagonal, first, count):
        rows = pl.ds(first, count)
        keys = jnp.concatenate([lt[spot, 0], lt[spot, 1]], axis=1)
        scores = dot(qa[rows], keys, ((1,), (0,))) * ((NOPE + ROPE) ** -0.5 * LOG2E)
        if diagonal:
            key_pos = lax.broadcasted_iota(jnp.int32, (count, 256), 1)
            query_pos = k * BLOCK + lax.broadcasted_iota(jnp.int32, (count, 256), 0) % BLOCK
            scores = jnp.where(key_pos <= query_pos, scores, MASKED)
            new_max = jnp.broadcast_to(jnp.max(scores, axis=1, keepdims=True), (count, 128))
        else:
            new_max = jnp.maximum(m_s[rows], jnp.max(scores, axis=1, keepdims=True))
        exps = jnp.exp2(scores - jnp.concatenate([new_max] * 2, axis=1))
        sums = exps[:, :128] + exps[:, 128:]
        weighted = dot(exps.astype(BF16), keys[:LAT], ((1,), (1,)))
        if diagonal:
            l_s[rows] = sums
            acc[rows] = weighted
        else:
            rescale = jnp.exp2(m_s[rows] - new_max)
            l_s[rows] = l_s[rows] * rescale + sums
            acc[rows] = acc[rows] * jnp.concatenate([rescale] * 4, axis=1) + weighted
        m_s[rows] = new_max

    def visit(dx, flip, first=0, count=1024):
        spot = place(dx, flip)

        @pl.when(spot < here)
        def _():
            attend(spot, False, first, count)

    arrive1(14)
    attend(here, True, 0, 1024)
    arrive1(2)
    start1(10)
    arrive1(4)
    start1(11)
    arrive1(0)
    start1(6, 9)
    arrive1(1)
    start1(8, 7, 15)
    arrive1(3, 5)
    start1(16, 17)
    arrive1(15)
    visit(0, True)
    arrive1(16)
    visit(3, False)
    arrive1(6)
    start1(12)
    arrive1(8)
    start1(13)
    arrive1(10, 11)
    start1(20)
    arrive1(17)
    visit(1, False)
    arrive1(7, 9)
    start1(18, 19)
    arrive1(20)
    visit(2, False)
    arrive1(12, 13)
    start1(21)
    arrive1(18)
    visit(3, True)
    arrive1(19)
    visit(1, True)
    arrive1(21)
    local[4].wait()

    mine = jnp.where(k == yl, here, 8)

    def swap(half, outgoing):
        return pltpu.make_async_remote_copy(
            src_ref=att.at[8, k, half], dst_ref=att.at[here, (1 - k) if outgoing else k, half],
            send_sem=swap_send.at[half], recv_sem=swap_recv.at[half], device_id=y_cross, device_id_type=MESH,
        )

    def cross(half):
        return pltpu.make_async_remote_copy(
            src_ref=att.at[8, k, half], dst_ref=att.at[here, 1 - k, half], send_sem=p3_send.at[half],
            recv_sem=p3_recv.at[half], device_id=y_near_cross, device_id_type=MESH,
        )

    for half in range(2):
        visit(2, True, 512 * half, 512)

        for i in range(4):
            rows = pl.ds(512 * half + i * BLOCK, BLOCK)
            normed = (acc[rows] / jnp.sum(l_s[rows], axis=1, keepdims=True)).astype(BF16)
            v = (4 * half + i) * VD
            att[mine, k, half, :, i * VD : (i + 1) * VD] = dot(normed, vu_v[:, v : v + VD], ((1,), (0,))).astype(BF16)

        @pl.when(k == yl)
        def _():
            if half == 0:
                start3(2, 5, 0)
            else:
                start3(3, 4, 1, 14)

        @pl.when(k != yl)
        def _():
            swap(half, True).start()
            cross(half).start()

    w_copy(1).start()

    @pl.when(k != yl)
    def _():
        swap(0, False).wait_recv()
        start3(2, 5)
        swap(1, False).wait_recv()
        start3(3, 4, 14)

    rounds = (
        (place(0), place(0, True)), (place(3), place(1)),
        (place(2),), (place(3, True), place(1, True)), (place(2, True),),
    )

    def project(r, slot):
        spot = rounds[r][slot]
        product = sum(
            dot(att[spot, s, half], wt[s, :, half * 512 : half * 512 + 512], ((1,), (1,)))
            for s in range(2) for half in range(2)
        )
        for zd in range(8):
            piece = product[zd * 16 : zd * 16 + 16]
            part[r, zd, slot * 16 : slot * 16 + 16] = piece
            if r >= 2:
                direct[r - 2, zd, slot * 16 : slot * 16 + 16] = piece.astype(BF16)

    def rs_copy(r, t, d):
        e = r * 8 + t * 2 + d
        rows = pl.ds(0, 32) if t else pl.ds(16 * d, 16)
        return pltpu.make_async_remote_copy(
            src_ref=sbuf.at[e, rows], dst_ref=rbuf.at[e, rows], send_sem=rs_send.at[e],
            recv_sem=rs_recv.at[e], device_id=(zp, zm)[d], device_id_type=MESH,
        )

    def rs_step(r, t):
        for d in range(2):
            e = r * 8 + t * 2 + d
            dest = (z + 4 - t) % 8 if d == 0 else (z + 4 + t) % 8
            if t == 0:
                rows = pl.ds(16 * d, 16)
                sbuf[e, rows] = part[r, dest, rows].astype(BF16)
            else:
                rs_copy(r, t - 1, d).wait_recv()
                if t == 1:
                    add, own = pl.ds(16 * d, 16), pl.ds(16 - 16 * d, 16)
                    sbuf[e, add] = (part[r, dest, add] + rbuf[e - 2, add].astype(F32)).astype(BF16)
                    sbuf[e, own] = part[r, dest, own].astype(BF16)
                else:
                    sbuf[e] = (part[r, dest] + rbuf[e - 2].astype(F32)).astype(BF16)
            rs_copy(r, t, d).start()

    def d_copy(r, i):
        rows = pl.ds(0, 16 * len(rounds[r]))
        return pltpu.make_async_remote_copy(
            src_ref=direct.at[r - 2, (z + i) % 8, rows], dst_ref=dbuf.at[r - 2, i - 1, rows], send_sem=d_send.at[r - 2, i - 1],
            recv_sem=d_recv.at[r - 2, i - 1], device_id=(c, ((z + i) % 8) * 2 + yl), device_id_type=MESH,
        )

    def spread(r):
        for i in (4, 3, 5, 2, 6, 1, 7):
            d_copy(r, i).start()

    def a_copy(r, slot, y2):
        e = r * 4 + slot * 2 + y2
        at = slot * 16 + y2 * 8
        return pltpu.make_async_remote_copy(
            src_ref=fin.at[r, pl.ds(at, 8)], dst_ref=landed.at[c], send_sem=a_send.at[e],
            recv_sem=a_recv.at[c], device_id=(rounds[r][slot] * 2 + yl, z * 2 + y2), device_id_type=MESH,
        )

    def finish(r):
        n = 16 * len(rounds[r])
        if r < 2:
            rs_copy(r, 3, 0).wait_recv()
            rs_copy(r, 3, 1).wait_recv()
            fin[r] = part[r, z] + rbuf[r * 8 + 6].astype(F32) + rbuf[r * 8 + 7].astype(F32)
        else:
            total = part[r, z, :n]
            for i in range(1, 8):
                d_copy(r, i).wait_recv()
                total = total + dbuf[r - 2, i - 1, :n].astype(F32)
            fin[r, :n] = total
        for slot in range(len(rounds[r])):
            for y2 in range(2):
                if r == 0 and slot == 0:
                    self_copy = (k == yl) & (yl == y2)

                    @pl.when(jnp.logical_not(self_copy))
                    def _():
                        a_copy(r, slot, y2).start()

                    @pl.when(self_copy)
                    def _():
                        landed[c] = fin[r, y2 * 8 : y2 * 8 + 8]
                else:
                    a_copy(r, slot, y2).start()

    arrive3(2)
    start3(10)
    arrive3(0)
    start3(6, 9)
    arrive3(4)
    start3(11)
    arrive3(1)
    start3(7, 8, 15)
    arrive3(3, 5)
    start3(16, 17)
    drain1()
    w_copy(0).wait_recv()
    w_copy(1).wait_recv()
    arrive3(14)
    project(0, 0)
    arrive3(15)
    project(0, 1)
    rs_step(0, 0)
    arrive3(10, 11)
    start3(20)
    arrive3(16, 17)
    project(1, 0)
    project(1, 1)
    rs_step(1, 0)
    rs_step(0, 1)
    arrive3(20)
    project(2, 0)
    spread(2)
    rs_step(1, 1)
    rs_step(0, 2)
    arrive3(6)
    start3(12)
    arrive3(8)
    start3(13)
    arrive3(7, 9)
    start3(18, 19)
    rs_step(1, 2)
    rs_step(0, 3)
    arrive3(18, 19)
    project(3, 0)
    project(3, 1)
    spread(3)
    arrive3(12, 13)
    start3(21)
    rs_step(1, 3)
    finish(0)
    arrive3(21)
    project(4, 0)
    spread(4)
    finish(1)
    finish(2)
    drain3()
    w_copy(0).wait_send()
    w_copy(1).wait_send()

    @pl.when(k != yl)
    def _():
        swap(0, True).wait_send()
        swap(1, True).wait_send()

    for r in range(2):
        for t in range(4):
            for d in range(2):
                rs_copy(r, t, d).wait_send()
    for i in range(1, 8):
        d_copy(2, i).wait_send()
    finish(3)
    finish(4)

    for c2 in range(16):

        @pl.when(jnp.logical_or(c != c2, yl != k))
        def _():
            pltpu.make_async_remote_copy(
                src_ref=landed.at[c2], dst_ref=landed.at[c2], send_sem=a_send.at[c2],
                recv_sem=a_recv.at[c2], device_id=core, device_id_type=MESH,
            ).wait_recv()

    out_ref[...] = jnp.concatenate([landed[c2] for c2 in range(16)], axis=1).astype(BF16)

    for r in range(5):
        if r >= 3:
            for i in range(1, 8):
                d_copy(r, i).wait_send()
        for slot in range(len(rounds[r])):
            for y2 in range(2):

                @pl.when(jnp.logical_not((k == yl) & (yl == y2) & (r == 0) & (slot == 0)))
                def _():
                    a_copy(r, slot, y2).wait_send()


def local(queries, query_rope, latent_cache, key_up, value_up, out_proj):
    dma = pltpu.SemaphoreType.DMA
    return pl.pallas_call(
        kernel,
        out_shape=jax.ShapeDtypeStruct((8, 7168), BF16),
        in_specs=[pl.BlockSpec(memory_space=pl.ANY)] * 6,
        out_specs=pl.BlockSpec(memory_space=pltpu.VMEM),
        scratch_shapes=[
            pltpu.VMEM((BLOCK, HEADS, NOPE), BF16),
            pltpu.VMEM((HEADS, ROPE, BLOCK), BF16),
            pltpu.VMEM((LAT, HEADS * NOPE), BF16),
            pltpu.VMEM((LAT, HEADS * VD), BF16),
            pltpu.VMEM((2, COLS, HEADS * VD), BF16),
            pltpu.VMEM((BLOCK * HEADS, NOPE), F32),
            pltpu.VMEM((HEADS * BLOCK, LAT + ROPE), BF16),
            pltpu.VMEM((8, 2, LAT + ROPE, BLOCK), BF16),
            pltpu.VMEM((HEADS * BLOCK, 128), F32),
            pltpu.VMEM((HEADS * BLOCK, 128), F32),
            pltpu.VMEM((HEADS * BLOCK, LAT), F32),
            pltpu.VMEM((9, 2, 2, BLOCK, HEADS * VD // 2), BF16),
            pltpu.VMEM((5, 8, 32, COLS), F32),
            pltpu.VMEM((3, 8, 32, COLS), BF16),
            pltpu.VMEM((16, 32, COLS), BF16),
            pltpu.VMEM((16, 32, COLS), BF16),
            pltpu.VMEM((3, 7, 32, COLS), BF16),
            pltpu.VMEM((5, 32, COLS), F32),
            pltpu.VMEM((16, 8, COLS), F32),
            dma((6,)), dma((4,)), dma((22,)), dma((22,)), dma((22,)), dma((22,)), dma((2,)), dma((2,)),
            dma((16,)), dma((16,)), dma((3, 7)), dma((3, 7)), dma((20,)), dma((16,)),
        ],
        compiler_params=pltpu.CompilerParams(
            collective_id=0, has_side_effects=True, vmem_limit_bytes=63 * 1024 * 1024
        ),
    )(queries, query_rope.transpose(1, 2, 0), latent_cache.T, key_up, value_up, out_proj.T)


def solution(mesh):
    placed = (
        P("ctx", "head", None),
        P("ctx", "head", None),
        P("ctx", None),
        P(None, "head"),
        P(None, "head"),
        P("head", "ctx"),
    )
    return jax.shard_map(
        local, mesh=mesh, in_specs=placed, out_specs=P(("ctx", "head"), None), check_vma=False
    )
```

time: 84.2 us -> 75.3 us (0.89)
  Pallas kernels: 82.5 us -> 73.2 us
    pallas_call x1, Pallas kernels: 82.5 us -> 73.2 us  [local(): pl.pallas_call(kernel, out_shape=jax.ShapeDtypeStruct((8, 7168), BF16), i...]
where the time goes in v2:
time: 75.3 us; the launch traced here: 74.8 us
  Pallas kernels  73.2 us (97%)
  local copies, waits for them, and re-layouts  1.55 us (2%)
    pallas_call x1, Pallas kernels, local(): pl.pallas_call(kernel, out_shape=jax.ShapeDtypeStruct((8, 7168), BF16), i...  73.2 us
    unnamed x1, local copies, waits for them, and re-layouts  1.55 us

profile of v2, /device:TPU:1, one launch (start us, length us, event | category | flops | bytes accessed | tf_op | source)
XLA Modules:
  0.0 74.8 jit_solution(4758896059371841029)
XLA Ops:
  0.0 73.2 %shard_map.64 = bf16[8,7168]{1,0:T(8,128)(2,1)} custom-call(bf16[128,8,128]{2,1,0:T(8,128)(2,1)} %q_hbm.1, bf16[8,64,128]{2,1,0:T(8,128)(2,1)} %bitcast.5, bf16[576,128]{1,0:T(8,128)(2,1)} %bitcast.4, bf16[512,1024]{1,0:T(8,128)(2,1)} %ku_hbm.1, bf16[512,1024]{1,0:T(8,128)(2,1)} %vu_hbm.1, bf16[448,1024]{1,0:T(8,128)(2,1)} %bitcast.3), custom_call_target="tpu_custom_call" | custom-call | tf_op jit(solution)/shard_map/pallas_call | solution.py:442
  73.2 1.6 %copy.8 = bf16[8,7168]{1,0:T(8,128)(2,1)} copy(bf16[8,7168]{1,0:T(8,128)(2,1)} %shard_map.64) | data formatting | bytes 229376

commit v3 on v2

--- a/solution.py
+++ b/solution.py
@@ -207,9 +207,9 @@
     arrive1(12, 13)
     start1(21)
     arrive1(18)
-    visit(3, True)
+    visit(3, True, 0, 512)
     arrive1(19)
-    visit(1, True)
+    visit(1, True, 0, 512)
     arrive1(21)
     local[4].wait()
 
@@ -228,6 +228,9 @@
         )
 
     for half in range(2):
+        if half == 1:
+            visit(3, True, 512, 512)
+            visit(1, True, 512, 512)
         visit(2, True, 512 * half, 512)
 
         for i in range(4):
@@ -245,8 +248,8 @@
 
         @pl.when(k != yl)
         def _():
+            cross(half).start()
             swap(half, True).start()
-            cross(half).start()
 
     w_copy(1).start()
 
@@ -263,16 +266,21 @@
     )
 
     def project(r, slot):
-        spot = rounds[r][slot]
-        product = sum(
-            dot(att[spot, s, half], wt[s, :, half * 512 : half * 512 + 512], ((1,), (1,)))
-            for s in range(2) for half in range(2)
-        )
-        for zd in range(8):
-            piece = product[zd * 16 : zd * 16 + 16]
-            part[r, zd, slot * 16 : slot * 16 + 16] = piece
-            if r >= 2:
-                direct[r - 2, zd, slot * 16 : slot * 16 + 16] = piece.astype(BF16)
+        if slot + 1 < len(rounds[r]) and r in (1, 3):
+            return
+        both = rounds[r] if r in (1, 3) else (rounds[r][slot],)
+        product = 0.0
+        for s in range(2):
+            for half in range(2):
+                rows = jnp.concatenate([att[spot, s, half] for spot in both], axis=0)
+                product = product + dot(rows, wt[s, :, half * 512 : half * 512 + 512], ((1,), (1,)))
+        for j in range(len(both)):
+            to = (j if r in (1, 3) else slot) * 16
+            for zd in range(8):
+                piece = product[j * BLOCK + zd * 16 : j * BLOCK + zd * 16 + 16]
+                part[r, zd, to : to + 16] = piece
+                if r >= 2:
+                    direct[r - 2, zd, to : to + 16] = piece.astype(BF16)
 
     def rs_copy(r, t, d):
         e = r * 8 + t * 2 + d
@@ -414,6 +422,17 @@
     finish(3)
     finish(4)
 
+    for r in range(5):
+        if r >= 3:
+            for i in range(1, 8):
+                d_copy(r, i).wait_send()
+        for slot in range(len(rounds[r])):
+            for y2 in range(2):
+
+                @pl.when(jnp.logical_not((k == yl) & (yl == y2) & (r == 0) & (slot == 0)))
+                def _():
+                    a_copy(r, slot, y2).wait_send()
+
     for c2 in range(16):
 
         @pl.when(jnp.logical_or(c != c2, yl != k))
@@ -424,17 +443,6 @@
             ).wait_recv()
 
     out_ref[...] = jnp.concatenate([landed[c2] for c2 in range(16)], axis=1).astype(BF16)
-
-    for r in range(5):
-        if r >= 3:
-            for i in range(1, 8):
-                d_copy(r, i).wait_send()
-        for slot in range(len(rounds[r])):
-            for y2 in range(2):
-
-                @pl.when(jnp.logical_not((k == yl) & (yl == y2) & (r == 0) & (slot == 0)))
-                def _():
-                    a_copy(r, slot, y2).wait_send()
 
 
 def local(queries, query_rope, latent_cache, key_up, value_up, out_proj):

time: 75.3 us -> 74.6 us (level)
  no operation moved by 1% of the time
where the time goes in v3:
time: 74.6 us; the launch traced here: 74.5 us
  Pallas kernels  73 us (98%)
  local copies, waits for them, and re-layouts  1.55 us (2%)
    pallas_call x1, Pallas kernels, local(): pl.pallas_call(kernel, out_shape=jax.ShapeDtypeStruct((8, 7168), BF16), i...  73 us
    unnamed x1, local copies, waits for them, and re-layouts  1.55 us

profile of v3, /device:TPU:1, one launch (start us, length us, event | category | flops | bytes accessed | tf_op | source)
XLA Modules:
  0.0 74.5 jit_solution(16391871867104454532)
XLA Ops:
  0.0 73.0 %shard_map.64 = bf16[8,7168]{1,0:T(8,128)(2,1)} custom-call(bf16[128,8,128]{2,1,0:T(8,128)(2,1)} %q_hbm.1, bf16[8,64,128]{2,1,0:T(8,128)(2,1)} %bitcast.5, bf16[576,128]{1,0:T(8,128)(2,1)} %bitcast.4, bf16[512,1024]{1,0:T(8,128)(2,1)} %ku_hbm.1, bf16[512,1024]{1,0:T(8,128)(2,1)} %vu_hbm.1, bf16[448,1024]{1,0:T(8,128)(2,1)} %bitcast.3), custom_call_target="tpu_custom_call" | custom-call | tf_op jit(solution)/shard_map/pallas_call | solution.py:450
  73.0 1.6 %copy.8 = bf16[8,7168]{1,0:T(8,128)(2,1)} copy(bf16[8,7168]{1,0:T(8,128)(2,1)} %shard_map.64) | data formatting | bytes 229376

commit v4 on v3

--- a/solution.py
+++ b/solution.py
@@ -62,11 +62,24 @@
     zm = (c, ((z + 7) % 8) * 2 + yl)
 
     barrier = pltpu.get_barrier_semaphore()
-    greeted = [((c + i) % 16, h) for i in range(1, 16)]
-    greeted += [((c + i) % 16, z * 2 + 1 - yl) for i in range(16)]
-    greeted += [(c, ((z + i) % 8) * 2 + yl) for i in range(1, 8)]
-    for peer in greeted:
-        pl.semaphore_signal(barrier, inc=1, device_id=peer, device_id_type=MESH)
+    stays = k == yl
+
+    def greet(peers):
+        for peer in peers:
+            pl.semaphore_signal(barrier, inc=1, device_id=peer, device_id_type=MESH)
+
+    def along(first, head):
+        return [((c + i) % 16, head) for i in range(first, 16, 2)]
+
+    greet(along(1, h) + along(0, z * 2 + 1 - yl) + [(c, ((z + i) % 8) * 2 + yl) for i in range(1, 8)])
+
+    @pl.when(stays)
+    def _():
+        greet(along(2, h))
+
+    @pl.when(jnp.logical_not(stays))
+    def _():
+        greet(along(1, z * 2 + 1 - yl) + [xp, xm, y_far])
 
     local[1].wait()
     local[2].wait()
@@ -81,7 +94,13 @@
     local[0].wait()
     local[5].wait()
 
-    pl.semaphore_wait(barrier, len(greeted))
+    @pl.when(stays)
+    def _():
+        pl.semaphore_wait(barrier, 30)
+
+    @pl.when(jnp.logical_not(stays))
+    def _():
+        pl.semaphore_wait(barrier, 34)
 
     def gather(at, send, recv, y_peer, last):
         LO, HI, ALL = 0, 1, None
@@ -131,11 +150,11 @@
         return att.at[i, s] if half is None else att.at[i, s, half]
 
     by_x = [(place(3, True), 0, xp, place(2, True)), (place(1, True), 1, xm, place(2, True))]
-    by_y = [(place(2), 0, y_far, place(2, True)), (place(2), 1, y_far, place(2, True))]
+    by_both = [(place(3, True), 0, xp, place(2, True)), (place(2), 1, y_far, place(2, True))]
     start1, arrive1, drain1 = gather(latent_at, p1_send, p1_recv, y_near, by_x)
-    start3, arrive3, drain3 = gather(att_at, p3_send, p3_recv, y_far, by_x)
-
-    start1(2, 4, 0, 3, 5, 1, 14)
+    start3, arrive3, drain3 = gather(att_at, p3_send, p3_recv, y_far, by_both)
+
+    start1(0, 2, 4, 1, 3, 5, 14)
 
     def w_copy(i):
         rows = (pl.ds(0, 384), pl.ds(384, 64))[i]
@@ -371,7 +390,9 @@
     arrive3(15)
     project(0, 1)
     rs_step(0, 0)
-    arrive3(10, 11)
+    arrive3(11)
+    start3(13)
+    arrive3(10)
     start3(20)
     arrive3(16, 17)
     project(1, 0)
@@ -385,9 +406,7 @@
     rs_step(0, 2)
     arrive3(6)
     start3(12)
-    arrive3(8)
-    start3(13)
-    arrive3(7, 9)
+    arrive3(8, 7, 9)
     start3(18, 19)
     rs_step(1, 2)
     rs_step(0, 3)

time: 74.6 us -> 74.7 us (level)
  no operation moved by 1% of the time
where the time goes in v4:
time: 74.7 us; the launch traced here: 74.6 us
  Pallas kernels  73 us (98%)
  local copies, waits for them, and re-layouts  1.55 us (2%)
    pallas_call x1, Pallas kernels, local(): pl.pallas_call(kernel, out_shape=jax.ShapeDtypeStruct((8, 7168), BF16), i...  73 us
    unnamed x1, local copies, waits for them, and re-layouts  1.55 us

profile of v4, /device:TPU:1, one launch (start us, length us, event | category | flops | bytes accessed | tf_op | source)
XLA Modules:
  0.0 74.6 jit_solution(13353578067547844673)
XLA Ops:
  0.0 73.0 %shard_map.64 = bf16[8,7168]{1,0:T(8,128)(2,1)} custom-call(bf16[128,8,128]{2,1,0:T(8,128)(2,1)} %q_hbm.1, bf16[8,64,128]{2,1,0:T(8,128)(2,1)} %bitcast.5, bf16[576,128]{1,0:T(8,128)(2,1)} %bitcast.4, bf16[512,1024]{1,0:T(8,128)(2,1)} %ku_hbm.1, bf16[512,1024]{1,0:T(8,128)(2,1)} %vu_hbm.1, bf16[448,1024]{1,0:T(8,128)(2,1)} %bitcast.3), custom_call_target="tpu_custom_call" | custom-call | tf_op jit(solution)/shard_map/pallas_call | solution.py:469
  73.1 1.6 %copy.8 = bf16[8,7168]{1,0:T(8,128)(2,1)} copy(bf16[8,7168]{1,0:T(8,128)(2,1)} %shard_map.64) | data formatting | bytes 229376
